TPU v7x, 512 devices: a whole 4x4x16 slice. The times are simulated.
512 devices in a mesh: dp: 4 (over x), ctx: 16 (over z), tp: 8 (over y, core).
Axes of the slice: x: 4, y: 4, z: 16, core: 2. Of those that a mesh axis runs over, the one named last changes fastest.
Arguments:
- inputs: bfloat16 [4, 4096, 8192], P('dp', 'ctx', 'tp'), may hold values from -6 to 6
- cotangent: bfloat16 [4, 4096, 8192], P('dp', 'ctx', 'tp'), may hold values from -6 to 6
- residues: float32 [512, 16], P('tp'), may hold values from -3 to 3
- decay_rates: float32 [512, 16], P('tp'), may hold values from 4.8828125e-05 to 0.0333333333
- skip_gain: float32 [8192], P('tp'), may hold values from -1 to 1
Outputs:
- outputs: bfloat16 [4, 4096, 8192], P('dp', 'ctx', 'tp')
- grad_inputs: bfloat16 [4, 4096, 8192], P('dp', 'ctx', 'tp')
- grad_residues: float32 [512, 16], P('tp')
- grad_skip: float32 [8192], P('tp')
All inputs are finite; a program needn't handle non-finite values.
Results may differ from a plain program's by a relative error of at most 0.0014.
Values sent between devices are 32-bit elements; how exact they have to be, the bound alone decides.
A program may use at most 64 MiB of HBM per device.

v0:
```python
import math
import jax
import jax.numpy as jnp
from jax import lax
from jax.sharding import PartitionSpec as P

highest = lax.Precision.HIGHEST


def passed_along(value, axis, by):
    length = lax.axis_size(axis)
    pairs = [(i, i + by) for i in range(length) if 0 <= i + by < length]
    return lax.ppermute(value, axis, pairs)


def shards(inputs, cotangent, residues, decay_rates, skip_gain):
    local_batch, block_rows, channels = inputs.shape
    group_count, mode_count = residues.shape
    group_width = channels // group_count
    sub_rows = math.gcd(256, block_rows)
    sub_count = block_rows // sub_rows
    weight = jnp.sqrt(1.0 - jnp.exp(-2.0 * decay_rates))
    coefficient = residues * weight
    positions = jnp.arange(sub_rows, dtype=jnp.float32)
    center = (sub_rows - 1) / 2.0
    rate_cube = decay_rates[:, :, None]
    decay_down = jnp.exp(-rate_cube * (positions - center))
    decay_up = jnp.exp(rate_cube * (positions - center))
    from_start = jnp.exp(-rate_cube * positions)
    to_end = jnp.exp(-rate_cube * (sub_rows - 1.0 - positions))
    five_shape = (local_batch, sub_count, sub_rows, group_count, group_width)
    state_shape = (local_batch, mode_count, channels)
    state_split = (local_batch, mode_count, group_count, group_width)
    inputs_wide = inputs.astype(jnp.float32).reshape(five_shape)
    cotangent_wide = cotangent.astype(jnp.float32).reshape(five_shape)
    sub_ends = jnp.einsum("gmt,bktgc->kbmgc", to_end, inputs_wide, precision=highest)
    sub_starts = jnp.einsum("gmt,bktgc->kbmgc", from_start, cotangent_wide, precision=highest)
    device_end = sub_ends[0]
    device_start = sub_starts[sub_count - 1]
    end_states = device_end.reshape(state_shape)
    start_states = device_start.reshape(state_shape)
    channel_rates = jnp.repeat(decay_rates.T, group_width, axis=1) * float(block_rows)
    passing = jnp.exp(-channel_rates)

    def relay_turn(turn, carried):
        incoming_x, incoming_d = carried
        sent_x = incoming_x * passing + end_states
        sent_d = incoming_d * passing + start_states
        return (passed_along(sent_x, "ctx", 1), passed_along(sent_d, "ctx", -1))

    empty_states = jnp.zeros_like(end_states)
    state_before, state_after = lax.fori_loop(
        0, lax.axis_size("ctx") - 1, relay_turn, (empty_states, empty_states)
    )
    block_count = math.gcd(group_count, 16)
    per_block = group_count // block_count
    causal_mask = positions[:, None] >= positions[None, :]

    def by_groups(array):
        return array.reshape((block_count, per_block) + array.shape[1:])

    def data_blocks(array):
        return array.reshape(
            local_batch, sub_count, sub_rows, block_count, per_block, group_width
        ).transpose(3, 0, 1, 2, 4, 5)

    def local_block(pieces):
        coef_piece, down_piece, up_piece, weight_piece, wide_x, wide_d, half_x, half_d = pieces
        kernel = jnp.where(
            causal_mask,
            jnp.einsum("gm,gmt,gms->gts", coef_piece, down_piece, up_piece, precision=highest),
            0.0,
        )
        local_out = jnp.einsum("gts,bksgc->bktgc", kernel, wide_x, precision=highest)
        local_back = jnp.einsum("gts,bktgc->bksgc", kernel, wide_d, precision=highest)
        pairs = jnp.einsum("bktgc,bksgc->gts", half_d, half_x, preferred_element_type=jnp.float32)
        pairs = jnp.where(causal_mask, pairs, 0.0)
        local_grad = weight_piece * jnp.einsum(
            "gmt,gts,gms->gm", down_piece, pairs, up_piece, precision=highest
        )
        return (local_out, local_back, local_grad)

    half_inputs = inputs.reshape(five_shape)
    half_cotangent = cotangent.reshape(five_shape)
    block_out, block_back, block_grad = lax.map(
        local_block,
        (
            by_groups(coefficient),
            by_groups(decay_down),
            by_groups(decay_up),
            by_groups(weight),
            data_blocks(inputs_wide),
            data_blocks(cotangent_wide),
            data_blocks(half_inputs),
            data_blocks(half_cotangent),
        ),
    )
    local_out = block_out.transpose(1, 2, 3, 0, 4, 5).reshape(five_shape)
    local_back = block_back.transpose(1, 2, 3, 0, 4, 5).reshape(five_shape)
    local_grad = block_grad.reshape(group_count, mode_count)
    running = state_before.reshape(state_split)
    before_list = [running]
    running = state_after.reshape(state_split)
    after_list = [None] * sub_count
    after_list[0] = running
    before_stack = jnp.stack(before_list, axis=1)
    after_stack = jnp.stack(after_list, axis=1)
    first_weights = coefficient[:, :, None] * jnp.exp(-rate_cube * (positions + 1.0))
    last_weights = coefficient[:, :, None] * jnp.exp(-rate_cube * (sub_rows - positions))
    carried_out = jnp.einsum("gmt,bkmgc->bktgc", first_weights, before_stack, precision=highest)
    carried_back = jnp.einsum("gmt,bkmgc->bktgc", last_weights, after_stack, precision=highest)
    carried_grad = (
        weight
        * jnp.exp(-decay_rates)
        * jnp.einsum("kbmgc,bkmgc->gm", sub_starts, before_stack, precision=highest)
    )
    skip_wide = skip_gain.reshape(group_count, group_width)
    outputs = (
        (local_out + carried_out + skip_wide * inputs_wide)
        .reshape(local_batch, block_rows, channels)
        .astype(jnp.bfloat16)
    )
    grad_inputs = (
        (local_back + carried_back + skip_wide * cotangent_wide)
        .reshape(local_batch, block_rows, channels)
        .astype(jnp.bfloat16)
    )
    token_total = local_batch * block_rows * lax.axis_size("dp") * lax.axis_size("ctx")
    scale = 1.0 / math.sqrt(token_total)
    skip_local = jnp.sum(inputs_wide * cotangent_wide, axis=(0, 1, 2)).reshape(channels)
    grad_residues, grad_skip = lax.psum(
        ((local_grad + carried_grad) * scale, skip_local * scale), ("dp", "ctx")
    )
    return (outputs, grad_inputs, grad_residues, grad_skip)


def solution(mesh):
    placed = (P("dp", "ctx", "tp"), P("dp", "ctx", "tp"), P("tp", None), P("tp", None), P("tp"))
    return jax.shard_map(
        shards,
        mesh=mesh,
        in_specs=placed,
        out_specs=(P("dp", "ctx", "tp"), P("dp", "ctx", "tp"), P("tp", None), P("tp")),
        check_vma=False,
    )
```

profile of v0, /device:TPU:16, one launch (start us, length us, event | category | flops | bytes accessed | tf_op | source)
XLA Modules:
  0.0 629.1 jit_solution(2040821487755064121)
XLA Ops:
  6.7 172.4 %while.30 = (s32[]{:T(128)}, f32[16,1,1,256,4,16]{3,5,4,2,1,0:T(8,128)}, f32[16,1,1,256,4,16]{3,5,4,2,1,0:T(8,128)}, f32[16,4,16]{2,1,0:T(4,128)S(1)}, f32[16,1,...) while((s32[]{:T(128)}, ...), condition=%wide.region_1.0_spmd.clone.clone, body=%wide.region_0.0_spmd.clone.clone.sunk | while | flops 210354176 | bytes 6303369 | solution.py:85
  14.7 2.7 fusion.87
  25.4 2.7 fusion.87
  36.2 2.7 fusion.87
  47.0 2.7 fusion.87
  57.7 2.7 fusion.87
  79.3 2.7 fusion.87
  90.1 2.7 fusion.87
  100.9 2.7 fusion.87
  111.7 2.7 fusion.87
  122.4 2.7 fusion.87
  133.2 2.7 fusion.87
  144.0 2.7 fusion.87
  154.8 2.7 fusion.87
  176.3 2.7 fusion.87
  184.8 158.3 %while.29 = (s32[]{:T(128)}, f32[1,16,1024]{2,1,0:T(8,128)S(1)}, f32[1,16,1024]{2,1,0:T(8,128)S(1)}, f32[1,16,1024]{2,1,0:T(8,128)S(1)}, f32[1,16,1024]{2,1,0:T(8,128)S(1)}, /*index=5*/f32[16,64]{1,0:T(8,128)S(1)}, s32[]{:T(128)}) while((s32[]{:T(128)}, f32[1,16,1024]{2,1,0:T(8,128)S(1)}, f32[1,16,1024]{2,1,0:T(8,128)S(1)}, ...), condition=%wide.region_3.4_spmd.clone, body=%wide.region_2.3_spmd.clone.sunk | while | flops 65538 | bytes 1183901 | solution.py:52
  185.3 3.8 collective-permute-start
  191.0 4.3 collective-permute-done.1
  195.8 3.8 collective-permute-start
  201.5 5.3 collective-permute-done.1
  207.3 5.1 collective-permute-start
  214.3 4.3 collective-permute-done.1
  219.1 3.9 collective-permute-start
  224.9 4.3 collective-permute-done.1
  229.7 4.8 collective-permute-start
  236.3 4.3 collective-permute-done.1
  241.1 5.1 collective-permute-start
  248.1 4.3 collective-permute-done.1
  252.9 3.9 collective-permute-start
  259.0 4.4 collective-permute-done.1
  263.9 3.9 collective-permute-start
  269.7 4.3 collective-permute-done.1
  274.5 2.8 collective-permute-start
  279.2 4.3 collective-permute-done.1
  284.0 3.3 collective-permute-start
  289.2 4.3 collective-permute-done.1
  293.9 3.1 collective-permute-start
  299.0 4.3 collective-permute-done.1
  303.7 3.3 collective-permute-start
  308.9 4.3 collective-permute-done.1
  313.7 3.4 collective-permute-start
  319.1 4.6 collective-permute-done.1
  324.2 3.4 collective-permute-start
  329.5 4.3 collective-permute-done.1
  334.2 2.7 collective-permute-start
  338.9 4.3 collective-permute-done.1
  343.9 3.3 fusion.34
  353.2 275.2 %all-reduce = (f32[64,16]{1,0:T(8,128)S(1)}, f32[1024]{0:T(1024)}) all-reduce(f32[64,16]{1,0:T(8,128)S(1)} %add_multiply_fusion, f32[1024]{0:T(1024)S(1)} %broadcast_multiply_fusion), channel_id=1, replica_groups=mesh['dp'=4,'ctx'=16,'tp'=8] {'dp','ctx'}, use_global_device_ids=true, to_apply=%region_4.5 | all-reduce | flops 2048 | bytes 16384 | tf_op jit(solution)/shard_map/psum | solution.py:131
  (273 shorter events, 188.0 us)
Async XLA Ops:
  0.6 0.8 copy-start.6
  1.6 1.7 copy-start
  3.3 1.2 copy-start.1
  180.9 0.8 copy-start.3
  184.1 0.7 copy-start.5
  185.3 5.7 collective-permute-start
  189.1 6.2 collective-permute-start.1
  195.8 5.7 collective-permute-start
  199.6 7.2 %collective-permute-start.1 = (f32[1,16,1024]{2,1,0:T(8,128)S(1)}, f32[1,16,1024]{2,1,0:T(8,128)S(1)}, u32[]{:S(2)}, u32[]{:S(2)}) collective-permute-start(f32[1,16,1024]{2,1,0:T(8,128)S(1)} %get-tuple-element.351), channel_id=1, source_target_pairs={{8,0},{16,8},{24,16},{32,24},{40,32},{48,40},{56,48},{64,56},{72,6... | collective-permute-start | bytes 196616 | tf_op jit(solution)/shard_map/while/body/eval_jaxpr/ppermute | solution.py:13
  207.3 7.0 %collective-permute-start = (f32[1,16,1024]{2,1,0:T(8,128)S(1)}, f32[1,16,1024]{2,1,0:T(8,128)S(1)}, u32[]{:S(2)}, u32[]{:S(2)}) collective-permute-start(f32[1,16,1024]{2,1,0:T(8,128)S(1)} %get-tuple-element.350), channel_id=1, source_target_pairs={{0,8},{8,16},{16,24},{24,32},{32,40},{40,48},{48,56},{56,64},{64,7... | collective-permute-start | bytes 196616 | tf_op jit(solution)/shard_map/while/body/eval_jaxpr/ppermute | solution.py:13
  212.4 6.2 collective-permute-start.1
  219.1 5.8 collective-permute-start
  223.0 6.2 collective-permute-start.1
  229.7 6.6 %collective-permute-start = (f32[1,16,1024]{2,1,0:T(8,128)S(1)}, f32[1,16,1024]{2,1,0:T(8,128)S(1)}, u32[]{:S(2)}, u32[]{:S(2)}) collective-permute-start(f32[1,16,1024]{2,1,0:T(8,128)S(1)} %get-tuple-element.350), channel_id=1, source_target_pairs={{0,8},{8,16},{16,24},{24,32},{32,40},{40,48},{48,56},{56,64},{64,7... | collective-permute-start | bytes 196616 | tf_op jit(solution)/shard_map/while/body/eval_jaxpr/ppermute | solution.py:13
  234.4 6.2 collective-permute-start.1
  241.1 7.0 %collective-permute-start = (f32[1,16,1024]{2,1,0:T(8,128)S(1)}, f32[1,16,1024]{2,1,0:T(8,128)S(1)}, u32[]{:S(2)}, u32[]{:S(2)}) collective-permute-start(f32[1,16,1024]{2,1,0:T(8,128)S(1)} %get-tuple-element.350), channel_id=1, source_target_pairs={{0,8},{8,16},{16,24},{24,32},{32,40},{40,48},{48,56},{56,64},{64,7... | collective-permute-start | bytes 196616 | tf_op jit(solution)/shard_map/while/body/eval_jaxpr/ppermute | solution.py:13
  246.2 6.2 collective-permute-start.1
  252.9 6.1 collective-permute-start
  256.8 6.6 %collective-permute-start.1 = (f32[1,16,1024]{2,1,0:T(8,128)S(1)}, f32[1,16,1024]{2,1,0:T(8,128)S(1)}, u32[]{:S(2)}, u32[]{:S(2)}) collective-permute-start(f32[1,16,1024]{2,1,0:T(8,128)S(1)} %get-tuple-element.351), channel_id=1, source_target_pairs={{8,0},{16,8},{24,16},{32,24},{40,32},{48,40},{56,48},{64,56},{72,6... | collective-permute-start | bytes 196616 | tf_op jit(solution)/shard_map/while/body/eval_jaxpr/ppermute | solution.py:13
  263.9 5.8 collective-permute-start
  267.8 6.2 collective-permute-start.1
  274.5 4.7 collective-permute-start
  277.3 6.2 collective-permute-start.1
  284.0 5.2 collective-permute-start
  287.3 6.2 collective-permute-start.1
  293.9 5.0 collective-permute-start
  297.1 6.2 collective-permute-start.1
  303.7 5.2 collective-permute-start
  307.0 6.2 collective-permute-start.1
  313.7 5.4 collective-permute-start
  317.1 6.5 %collective-permute-start.1 = (f32[1,16,1024]{2,1,0:T(8,128)S(1)}, f32[1,16,1024]{2,1,0:T(8,128)S(1)}, u32[]{:S(2)}, u32[]{:S(2)}) collective-permute-start(f32[1,16,1024]{2,1,0:T(8,128)S(1)} %get-tuple-element.351), channel_id=1, source_target_pairs={{8,0},{16,8},{24,16},{32,24},{40,32},{48,40},{56,48},{64,56},{72,6... | collective-permute-start | bytes 196616 | tf_op jit(solution)/shard_map/while/body/eval_jaxpr/ppermute | solution.py:13
  324.2 5.3 collective-permute-start
  327.6 6.2 collective-permute-start.1
  334.2 4.6 collective-permute-start
  337.0 6.2 collective-permute-start.1
  343.1 0.7 copy-start.7
  350.9 1.0 copy-start.4
  352.0 1.0 copy-start.2
where the time goes:
time: 634 us; the launch traced here: 629 us
  blocking collectives  275 us (43%)
  matrix products  163 us (26%)
  starting transfers between devices  75.9 us (12%)
  waiting for transfers between devices  74.7 us (12%)
  local copies, waits for them, and re-layouts  34.5 us (5%)
    psum x1, blocking collectives, shards(): lax.psum(((local_grad + carried_grad) * scale, skip_local * scale), ('dp'...  275 us
    ppermute x30, starting transfers between devices, passed_along(): return lax.ppermute(value, axis, pairs)  75.9 us
    ppermute x30, waiting for transfers between devices, passed_along(): return lax.ppermute(value, axis, pairs)  74.7 us
    dot_general x16, matrix products, local_block(): jnp.einsum('gmt,gts,gms->gm', down_piece, pairs, up_piece, precision=high...  43.6 us
    dot_general x16, matrix products, local_block(): jnp.einsum('gts,bksgc->bktgc', kernel, wide_x, precision=highest)  39.2 us
    dot_general x16, matrix products, local_block(): jnp.einsum('gm,gmt,gms->gts', coef_piece, down_piece, up_piece, precision...  32.7 us
    dot_general x16, matrix products, local_block(): jnp.einsum('gts,bktgc->bksgc', kernel, wide_d, precision=highest)  19.9 us
    dot_general x16, matrix products, local_block(): jnp.einsum('bktgc,bksgc->gts', half_d, half_x, preferred_element_type=jnp...  17.8 us
  transfers between devices with their start and end apart: 30, of which 30 were waited for; matrix products, arithmetic and copies ran while one was open for 0% of the time, Pallas kernels for 0%

commit v1 on v0

--- a/solution.py
+++ b/solution.py
@@ -129,7 +129,7 @@
     scale = 1.0 / math.sqrt(token_total)
     skip_local = jnp.sum(inputs_wide * cotangent_wide, axis=(0, 1, 2)).reshape(channels)
     grad_residues, grad_skip = lax.psum(
-        ((local_grad + carried_grad) * scale, skip_local * scale), ("dp", "ctx")
+        lax.psum(((local_grad + carried_grad) * scale, skip_local * scale), "dp"), "ctx"
     )
     return (outputs, grad_inputs, grad_residues, grad_skip)
 

time: 634 us -> 430 us (0.68)
  the two profiles are of different devices: /device:TPU:16 before, /device:TPU:8 now
where the time goes in v1:
time: 430 us; the launch traced here: 425 us
  matrix products  163 us (38%)
  starting transfers between devices  76 us (18%)
  waiting for transfers between devices  74.6 us (17%)
  blocking collectives  71.7 us (17%)
  local copies, waits for them, and re-layouts  33.9 us (8%)
    ppermute x30, starting transfers between devices, passed_along(): return lax.ppermute(value, axis, pairs)  76 us
    ppermute x30, waiting for transfers between devices, passed_along(): return lax.ppermute(value, axis, pairs)  74.6 us
    psum x1, blocking collectives, shards(): lax.psum(lax.psum(((local_grad + carried_grad) * scale, skip_local * scal...  54.3 us
    dot_general x16, matrix products, local_block(): jnp.einsum('gmt,gts,gms->gm', down_piece, pairs, up_piece, precision=high...  43.6 us
    dot_general x16, matrix products, local_block(): jnp.einsum('gts,bksgc->bktgc', kernel, wide_x, precision=highest)  39.2 us
    dot_general x16, matrix products, local_block(): jnp.einsum('gm,gmt,gms->gts', coef_piece, down_piece, up_piece, precision...  32.7 us
    dot_general x16, matrix products, local_block(): jnp.einsum('gts,bktgc->bksgc', kernel, wide_d, precision=highest)  19.9 us
    dot_general x16, matrix products, local_block(): jnp.einsum('bktgc,bksgc->gts', half_d, half_x, preferred_element_type=jnp...  17.8 us
  transfers between devices with their start and end apart: 30, of which 30 were waited for; matrix products, arithmetic and copies ran while one was open for 0% of the time, Pallas kernels for 0%

profile of v1, /device:TPU:8, one launch (start us, length us, event | category | flops | bytes accessed | tf_op | source)
XLA Modules:
  0.0 425.0 jit_solution(17886656757951972473)
XLA Ops:
  6.7 172.4 %while.30 = (s32[]{:T(128)}, f32[16,1,1,256,4,16]{3,5,4,2,1,0:T(8,128)}, f32[16,1,1,256,4,16]{3,5,4,2,1,0:T(8,128)}, f32[16,4,16]{2,1,0:T(4,128)S(1)}, f32[16,1,...) while((s32[]{:T(128)}, ...), condition=%wide.region_1.0_spmd.clone.clone, body=%wide.region_0.0_spmd.clone.clone.sunk | while | flops 210354176 | bytes 6303369 | solution.py:85
  14.7 2.7 fusion.87
  25.5 2.7 fusion.87
  36.2 2.7 fusion.87
  47.0 2.7 fusion.87
  57.8 2.7 fusion.87
  68.6 2.7 fusion.87
  90.1 2.7 fusion.87
  100.9 2.7 fusion.87
  122.5 2.7 fusion.87
  133.2 2.7 fusion.87
  144.0 2.7 fusion.87
  154.8 2.7 fusion.87
  165.6 2.7 fusion.87
  184.0 158.4 %while.29 = (s32[]{:T(128)}, f32[1,16,1024]{2,1,0:T(8,128)S(1)}, f32[1,16,1024]{2,1,0:T(8,128)S(1)}, f32[1,16,1024]{2,1,0:T(8,128)S(1)}, f32[1,16,1024]{2,1,0:T(8,128)S(1)}, /*index=5*/f32[16,64]{1,0:T(8,128)S(1)}, s32[]{:T(128)}) while((s32[]{:T(128)}, f32[1,16,1024]{2,1,0:T(8,128)S(1)}, f32[1,16,1024]{2,1,0:T(8,128)S(1)}, ...), condition=%wide.region_3.4_spmd.clone, body=%wide.region_2.3_spmd.clone.sunk | while | flops 65538 | bytes 1183901 | solution.py:52
  184.5 3.8 collective-permute-start
  190.2 4.3 %collective-permute-done.1 = f32[1,16,1024]{2,1,0:T(8,128)S(1)} collective-permute-done((f32[1,16,1024]{2,1,0:T(8,128)S(1)}, f32[1,16,1024]{2,1,0:T(8,128)S(1)}, u32[]{:S(2)}, u32[]{:S(2)}) %collective-permute-start.1) | collective-permute-done | bytes 65568 | tf_op jit(solution)/shard_map/while/body/eval_jaxpr/ppermute | solution.py:13
  195.0 3.8 collective-permute-start
  200.7 5.3 %collective-permute-done.1 = f32[1,16,1024]{2,1,0:T(8,128)S(1)} collective-permute-done((f32[1,16,1024]{2,1,0:T(8,128)S(1)}, f32[1,16,1024]{2,1,0:T(8,128)S(1)}, u32[]{:S(2)}, u32[]{:S(2)}) %collective-permute-start.1) | collective-permute-done | bytes 65568 | tf_op jit(solution)/shard_map/while/body/eval_jaxpr/ppermute | solution.py:13
  206.5 5.1 %collective-permute-start = (f32[1,16,1024]{2,1,0:T(8,128)S(1)}, f32[1,16,1024]{2,1,0:T(8,128)S(1)}, u32[]{:S(2)}, u32[]{:S(2)}) collective-permute-start(f32[1,16,1024]{2,1,0:T(8,128)S(1)} %get-tuple-element.352), channel_id=1, source_target_pairs={{0,8},{8,16},{16,24},{24,32},{32,40},{40,48},{48,56},{56,64},{64,7... | collective-permute-start | bytes 196616 | tf_op jit(solution)/shard_map/while/body/eval_jaxpr/ppermute | solution.py:13
  213.5 4.3 %collective-permute-done.1 = f32[1,16,1024]{2,1,0:T(8,128)S(1)} collective-permute-done((f32[1,16,1024]{2,1,0:T(8,128)S(1)}, f32[1,16,1024]{2,1,0:T(8,128)S(1)}, u32[]{:S(2)}, u32[]{:S(2)}) %collective-permute-start.1) | collective-permute-done | bytes 65568 | tf_op jit(solution)/shard_map/while/body/eval_jaxpr/ppermute | solution.py:13
  218.3 3.9 collective-permute-start
  224.1 4.3 %collective-permute-done.1 = f32[1,16,1024]{2,1,0:T(8,128)S(1)} collective-permute-done((f32[1,16,1024]{2,1,0:T(8,128)S(1)}, f32[1,16,1024]{2,1,0:T(8,128)S(1)}, u32[]{:S(2)}, u32[]{:S(2)}) %collective-permute-start.1) | collective-permute-done | bytes 65568 | tf_op jit(solution)/shard_map/while/body/eval_jaxpr/ppermute | solution.py:13
  228.9 4.8 %collective-permute-start = (f32[1,16,1024]{2,1,0:T(8,128)S(1)}, f32[1,16,1024]{2,1,0:T(8,128)S(1)}, u32[]{:S(2)}, u32[]{:S(2)}) collective-permute-start(f32[1,16,1024]{2,1,0:T(8,128)S(1)} %get-tuple-element.352), channel_id=1, source_target_pairs={{0,8},{8,16},{16,24},{24,32},{32,40},{40,48},{48,56},{56,64},{64,7... | collective-permute-start | bytes 196616 | tf_op jit(solution)/shard_map/while/body/eval_jaxpr/ppermute | solution.py:13
  235.6 4.3 %collective-permute-done.1 = f32[1,16,1024]{2,1,0:T(8,128)S(1)} collective-permute-done((f32[1,16,1024]{2,1,0:T(8,128)S(1)}, f32[1,16,1024]{2,1,0:T(8,128)S(1)}, u32[]{:S(2)}, u32[]{:S(2)}) %collective-permute-start.1) | collective-permute-done | bytes 65568 | tf_op jit(solution)/shard_map/while/body/eval_jaxpr/ppermute | solution.py:13
  240.3 5.1 %collective-permute-start = (f32[1,16,1024]{2,1,0:T(8,128)S(1)}, f32[1,16,1024]{2,1,0:T(8,128)S(1)}, u32[]{:S(2)}, u32[]{:S(2)}) collective-permute-start(f32[1,16,1024]{2,1,0:T(8,128)S(1)} %get-tuple-element.352), channel_id=1, source_target_pairs={{0,8},{8,16},{16,24},{24,32},{32,40},{40,48},{48,56},{56,64},{64,7... | collective-permute-start | bytes 196616 | tf_op jit(solution)/shard_map/while/body/eval_jaxpr/ppermute | solution.py:13
  247.4 4.3 %collective-permute-done.1 = f32[1,16,1024]{2,1,0:T(8,128)S(1)} collective-permute-done((f32[1,16,1024]{2,1,0:T(8,128)S(1)}, f32[1,16,1024]{2,1,0:T(8,128)S(1)}, u32[]{:S(2)}, u32[]{:S(2)}) %collective-permute-start.1) | collective-permute-done | bytes 65568 | tf_op jit(solution)/shard_map/while/body/eval_jaxpr/ppermute | solution.py:13
  252.1 3.9 collective-permute-start
  258.3 4.3 %collective-permute-done.1 = f32[1,16,1024]{2,1,0:T(8,128)S(1)} collective-permute-done((f32[1,16,1024]{2,1,0:T(8,128)S(1)}, f32[1,16,1024]{2,1,0:T(8,128)S(1)}, u32[]{:S(2)}, u32[]{:S(2)}) %collective-permute-start.1) | collective-permute-done | bytes 65568 | tf_op jit(solution)/shard_map/while/body/eval_jaxpr/ppermute | solution.py:13
  263.1 3.9 collective-permute-start
  268.9 4.3 %collective-permute-done.1 = f32[1,16,1024]{2,1,0:T(8,128)S(1)} collective-permute-done((f32[1,16,1024]{2,1,0:T(8,128)S(1)}, f32[1,16,1024]{2,1,0:T(8,128)S(1)}, u32[]{:S(2)}, u32[]{:S(2)}) %collective-permute-start.1) | collective-permute-done | bytes 65568 | tf_op jit(solution)/shard_map/while/body/eval_jaxpr/ppermute | solution.py:13
  273.7 2.8 collective-permute-start
  278.4 4.3 %collective-permute-done.1 = f32[1,16,1024]{2,1,0:T(8,128)S(1)} collective-permute-done((f32[1,16,1024]{2,1,0:T(8,128)S(1)}, f32[1,16,1024]{2,1,0:T(8,128)S(1)}, u32[]{:S(2)}, u32[]{:S(2)}) %collective-permute-start.1) | collective-permute-done | bytes 65568 | tf_op jit(solution)/shard_map/while/body/eval_jaxpr/ppermute | solution.py:13
  283.2 3.3 collective-permute-start
  288.4 4.3 %collective-permute-done.1 = f32[1,16,1024]{2,1,0:T(8,128)S(1)} collective-permute-done((f32[1,16,1024]{2,1,0:T(8,128)S(1)}, f32[1,16,1024]{2,1,0:T(8,128)S(1)}, u32[]{:S(2)}, u32[]{:S(2)}) %collective-permute-start.1) | collective-permute-done | bytes 65568 | tf_op jit(solution)/shard_map/while/body/eval_jaxpr/ppermute | solution.py:13
  293.1 3.1 collective-permute-start
  298.2 4.3 %collective-permute-done.1 = f32[1,16,1024]{2,1,0:T(8,128)S(1)} collective-permute-done((f32[1,16,1024]{2,1,0:T(8,128)S(1)}, f32[1,16,1024]{2,1,0:T(8,128)S(1)}, u32[]{:S(2)}, u32[]{:S(2)}) %collective-permute-start.1) | collective-permute-done | bytes 65568 | tf_op jit(solution)/shard_map/while/body/eval_jaxpr/ppermute | solution.py:13
  302.9 3.3 collective-permute-start
  308.2 4.3 %collective-permute-done.1 = f32[1,16,1024]{2,1,0:T(8,128)S(1)} collective-permute-done((f32[1,16,1024]{2,1,0:T(8,128)S(1)}, f32[1,16,1024]{2,1,0:T(8,128)S(1)}, u32[]{:S(2)}, u32[]{:S(2)}) %collective-permute-start.1) | collective-permute-done | bytes 65568 | tf_op jit(solution)/shard_map/while/body/eval_jaxpr/ppermute | solution.py:13
  312.9 3.4 collective-permute-start
  318.3 4.6 %collective-permute-done.1 = f32[1,16,1024]{2,1,0:T(8,128)S(1)} collective-permute-done((f32[1,16,1024]{2,1,0:T(8,128)S(1)}, f32[1,16,1024]{2,1,0:T(8,128)S(1)}, u32[]{:S(2)}, u32[]{:S(2)}) %collective-permute-start.1) | collective-permute-done | bytes 65568 | tf_op jit(solution)/shard_map/while/body/eval_jaxpr/ppermute | solution.py:13
  323.4 3.4 collective-permute-start
  328.7 4.3 %collective-permute-done.1 = f32[1,16,1024]{2,1,0:T(8,128)S(1)} collective-permute-done((f32[1,16,1024]{2,1,0:T(8,128)S(1)}, f32[1,16,1024]{2,1,0:T(8,128)S(1)}, u32[]{:S(2)}, u32[]{:S(2)}) %collective-permute-start.1) | collective-permute-done | bytes 65568 | tf_op jit(solution)/shard_map/while/body/eval_jaxpr/ppermute | solution.py:13
  333.5 2.8 collective-permute-start
  338.1 4.3 %collective-permute-done.1 = f32[1,16,1024]{2,1,0:T(8,128)S(1)} collective-permute-done((f32[1,16,1024]{2,1,0:T(8,128)S(1)}, f32[1,16,1024]{2,1,0:T(8,128)S(1)}, u32[]{:S(2)}, u32[]{:S(2)}) %collective-permute-start.1) | collective-permute-done | bytes 65568 | tf_op jit(solution)/shard_map/while/body/eval_jaxpr/ppermute | solution.py:13
  343.9 17.4 %all-reduce.1 = (f32[64,16]{1,0:T(8,128)S(1)}, f32[1024]{0:T(1024)S(1)}) all-reduce(f32[64,16]{1,0:T(8,128)S(1)} %add_multiply_fusion, f32[1024]{0:T(1024)S(1)} %broadcast_multiply_fusion), channel_id=1, replica_groups=mesh['dp'=4,'ctx'=16,'tp'=8] {'dp'}, use_global_device_ids=true, to_apply=%region_4.5 | all-reduce | flops 2048 | bytes 16384 | tf_op jit(solution)/shard_map/psum | solution.py:132
  361.2 54.3 %all-reduce = (f32[64,16]{1,0:T(8,128)S(1)}, f32[1024]{0:T(1024)}) all-reduce(f32[64,16]{1,0:T(8,128)S(1)} %get-tuple-element.243, f32[1024]{0:T(1024)S(1)} %get-tuple-element.244), channel_id=1, replica_groups=mesh['dp'=4,'ctx'=16,'tp'=8] {'ctx'}, use_global_device_ids=true, to_apply=%region_5.6 | all-reduce | flops 2048 | bytes 16384 | tf_op jit(solution)/shard_map/psum | solution.py:131
  417.0 3.3 fusion.34
  (270 shorter events, 190.2 us)
Async XLA Ops:
  0.6 0.8 copy-start.4
  1.6 1.7 copy-start
  3.3 1.2 copy-start.1
  183.3 0.7 copy-start.3
  184.5 5.7 %collective-permute-start = (f32[1,16,1024]{2,1,0:T(8,128)S(1)}, f32[1,16,1024]{2,1,0:T(8,128)S(1)}, u32[]{:S(2)}, u32[]{:S(2)}) collective-permute-start(f32[1,16,1024]{2,1,0:T(8,128)S(1)} %get-tuple-element.352), channel_id=1, source_target_pairs={{0,8},{8,16},{16,24},{24,32},{32,40},{40,48},{48,56},{56,64},{64,7... | collective-permute-start | bytes 196616 | tf_op jit(solution)/shard_map/while/body/eval_jaxpr/ppermute | solution.py:13
  188.4 6.2 %collective-permute-start.1 = (f32[1,16,1024]{2,1,0:T(8,128)S(1)}, f32[1,16,1024]{2,1,0:T(8,128)S(1)}, u32[]{:S(2)}, u32[]{:S(2)}) collective-permute-start(f32[1,16,1024]{2,1,0:T(8,128)S(1)} %get-tuple-element.353), channel_id=1, source_target_pairs={{8,0},{16,8},{24,16},{32,24},{40,32},{48,40},{56,48},{64,56},{72,6... | collective-permute-start | bytes 196616 | tf_op jit(solution)/shard_map/while/body/eval_jaxpr/ppermute | solution.py:13
  195.0 5.7 %collective-permute-start = (f32[1,16,1024]{2,1,0:T(8,128)S(1)}, f32[1,16,1024]{2,1,0:T(8,128)S(1)}, u32[]{:S(2)}, u32[]{:S(2)}) collective-permute-start(f32[1,16,1024]{2,1,0:T(8,128)S(1)} %get-tuple-element.352), channel_id=1, source_target_pairs={{0,8},{8,16},{16,24},{24,32},{32,40},{40,48},{48,56},{56,64},{64,7... | collective-permute-start | bytes 196616 | tf_op jit(solution)/shard_map/while/body/eval_jaxpr/ppermute | solution.py:13
  198.9 7.2 %collective-permute-start.1 = (f32[1,16,1024]{2,1,0:T(8,128)S(1)}, f32[1,16,1024]{2,1,0:T(8,128)S(1)}, u32[]{:S(2)}, u32[]{:S(2)}) collective-permute-start(f32[1,16,1024]{2,1,0:T(8,128)S(1)} %get-tuple-element.353), channel_id=1, source_target_pairs={{8,0},{16,8},{24,16},{32,24},{40,32},{48,40},{56,48},{64,56},{72,6... | collective-permute-start | bytes 196616 | tf_op jit(solution)/shard_map/while/body/eval_jaxpr/ppermute | solution.py:13
  206.5 7.0 %collective-permute-start = (f32[1,16,1024]{2,1,0:T(8,128)S(1)}, f32[1,16,1024]{2,1,0:T(8,128)S(1)}, u32[]{:S(2)}, u32[]{:S(2)}) collective-permute-start(f32[1,16,1024]{2,1,0:T(8,128)S(1)} %get-tuple-element.352), channel_id=1, source_target_pairs={{0,8},{8,16},{16,24},{24,32},{32,40},{40,48},{48,56},{56,64},{64,7... | collective-permute-start | bytes 196616 | tf_op jit(solution)/shard_map/while/body/eval_jaxpr/ppermute | solution.py:13
  211.7 6.2 %collective-permute-start.1 = (f32[1,16,1024]{2,1,0:T(8,128)S(1)}, f32[1,16,1024]{2,1,0:T(8,128)S(1)}, u32[]{:S(2)}, u32[]{:S(2)}) collective-permute-start(f32[1,16,1024]{2,1,0:T(8,128)S(1)} %get-tuple-element.353), channel_id=1, source_target_pairs={{8,0},{16,8},{24,16},{32,24},{40,32},{48,40},{56,48},{64,56},{72,6... | collective-permute-start | bytes 196616 | tf_op jit(solution)/shard_map/while/body/eval_jaxpr/ppermute | solution.py:13
  218.3 5.8 %collective-permute-start = (f32[1,16,1024]{2,1,0:T(8,128)S(1)}, f32[1,16,1024]{2,1,0:T(8,128)S(1)}, u32[]{:S(2)}, u32[]{:S(2)}) collective-permute-start(f32[1,16,1024]{2,1,0:T(8,128)S(1)} %get-tuple-element.352), channel_id=1, source_target_pairs={{0,8},{8,16},{16,24},{24,32},{32,40},{40,48},{48,56},{56,64},{64,7... | collective-permute-start | bytes 196616 | tf_op jit(solution)/shard_map/while/body/eval_jaxpr/ppermute | solution.py:13
  222.2 6.2 %collective-permute-start.1 = (f32[1,16,1024]{2,1,0:T(8,128)S(1)}, f32[1,16,1024]{2,1,0:T(8,128)S(1)}, u32[]{:S(2)}, u32[]{:S(2)}) collective-permute-start(f32[1,16,1024]{2,1,0:T(8,128)S(1)} %get-tuple-element.353), channel_id=1, source_target_pairs={{8,0},{16,8},{24,16},{32,24},{40,32},{48,40},{56,48},{64,56},{72,6... | collective-permute-start | bytes 196616 | tf_op jit(solution)/shard_map/while/body/eval_jaxpr/ppermute | solution.py:13
  228.9 6.7 %collective-permute-start = (f32[1,16,1024]{2,1,0:T(8,128)S(1)}, f32[1,16,1024]{2,1,0:T(8,128)S(1)}, u32[]{:S(2)}, u32[]{:S(2)}) collective-permute-start(f32[1,16,1024]{2,1,0:T(8,128)S(1)} %get-tuple-element.352), channel_id=1, source_target_pairs={{0,8},{8,16},{16,24},{24,32},{32,40},{40,48},{48,56},{56,64},{64,7... | collective-permute-start | bytes 196616 | tf_op jit(solution)/shard_map/while/body/eval_jaxpr/ppermute | solution.py:13
  233.7 6.2 %collective-permute-start.1 = (f32[1,16,1024]{2,1,0:T(8,128)S(1)}, f32[1,16,1024]{2,1,0:T(8,128)S(1)}, u32[]{:S(2)}, u32[]{:S(2)}) collective-permute-start(f32[1,16,1024]{2,1,0:T(8,128)S(1)} %get-tuple-element.353), channel_id=1, source_target_pairs={{8,0},{16,8},{24,16},{32,24},{40,32},{48,40},{56,48},{64,56},{72,6... | collective-permute-start | bytes 196616 | tf_op jit(solution)/shard_map/while/body/eval_jaxpr/ppermute | solution.py:13
  240.3 7.0 %collective-permute-start = (f32[1,16,1024]{2,1,0:T(8,128)S(1)}, f32[1,16,1024]{2,1,0:T(8,128)S(1)}, u32[]{:S(2)}, u32[]{:S(2)}) collective-permute-start(f32[1,16,1024]{2,1,0:T(8,128)S(1)} %get-tuple-element.352), channel_id=1, source_target_pairs={{0,8},{8,16},{16,24},{24,32},{32,40},{40,48},{48,56},{56,64},{64,7... | collective-permute-start | bytes 196616 | tf_op jit(solution)/shard_map/while/body/eval_jaxpr/ppermute | solution.py:13
  245.5 6.2 %collective-permute-start.1 = (f32[1,16,1024]{2,1,0:T(8,128)S(1)}, f32[1,16,1024]{2,1,0:T(8,128)S(1)}, u32[]{:S(2)}, u32[]{:S(2)}) collective-permute-start(f32[1,16,1024]{2,1,0:T(8,128)S(1)} %get-tuple-element.353), channel_id=1, source_target_pairs={{8,0},{16,8},{24,16},{32,24},{40,32},{48,40},{56,48},{64,56},{72,6... | collective-permute-start | bytes 196616 | tf_op jit(solution)/shard_map/while/body/eval_jaxpr/ppermute | solution.py:13
  252.1 6.1 %collective-permute-start = (f32[1,16,1024]{2,1,0:T(8,128)S(1)}, f32[1,16,1024]{2,1,0:T(8,128)S(1)}, u32[]{:S(2)}, u32[]{:S(2)}) collective-permute-start(f32[1,16,1024]{2,1,0:T(8,128)S(1)} %get-tuple-element.352), channel_id=1, source_target_pairs={{0,8},{8,16},{16,24},{24,32},{32,40},{40,48},{48,56},{56,64},{64,7... | collective-permute-start | bytes 196616 | tf_op jit(solution)/shard_map/while/body/eval_jaxpr/ppermute | solution.py:13
  256.1 6.6 %collective-permute-start.1 = (f32[1,16,1024]{2,1,0:T(8,128)S(1)}, f32[1,16,1024]{2,1,0:T(8,128)S(1)}, u32[]{:S(2)}, u32[]{:S(2)}) collective-permute-start(f32[1,16,1024]{2,1,0:T(8,128)S(1)} %get-tuple-element.353), channel_id=1, source_target_pairs={{8,0},{16,8},{24,16},{32,24},{40,32},{48,40},{56,48},{64,56},{72,6... | collective-permute-start | bytes 196616 | tf_op jit(solution)/shard_map/while/body/eval_jaxpr/ppermute | solution.py:13
  263.1 5.8 %collective-permute-start = (f32[1,16,1024]{2,1,0:T(8,128)S(1)}, f32[1,16,1024]{2,1,0:T(8,128)S(1)}, u32[]{:S(2)}, u32[]{:S(2)}) collective-permute-start(f32[1,16,1024]{2,1,0:T(8,128)S(1)} %get-tuple-element.352), channel_id=1, source_target_pairs={{0,8},{8,16},{16,24},{24,32},{32,40},{40,48},{48,56},{56,64},{64,7... | collective-permute-start | bytes 196616 | tf_op jit(solution)/shard_map/while/body/eval_jaxpr/ppermute | solution.py:13
  267.0 6.2 %collective-permute-start.1 = (f32[1,16,1024]{2,1,0:T(8,128)S(1)}, f32[1,16,1024]{2,1,0:T(8,128)S(1)}, u32[]{:S(2)}, u32[]{:S(2)}) collective-permute-start(f32[1,16,1024]{2,1,0:T(8,128)S(1)} %get-tuple-element.353), channel_id=1, source_target_pairs={{8,0},{16,8},{24,16},{32,24},{40,32},{48,40},{56,48},{64,56},{72,6... | collective-permute-start | bytes 196616 | tf_op jit(solution)/shard_map/while/body/eval_jaxpr/ppermute | solution.py:13
  273.7 4.7 %collective-permute-start = (f32[1,16,1024]{2,1,0:T(8,128)S(1)}, f32[1,16,1024]{2,1,0:T(8,128)S(1)}, u32[]{:S(2)}, u32[]{:S(2)}) collective-permute-start(f32[1,16,1024]{2,1,0:T(8,128)S(1)} %get-tuple-element.352), channel_id=1, source_target_pairs={{0,8},{8,16},{16,24},{24,32},{32,40},{40,48},{48,56},{56,64},{64,7... | collective-permute-start | bytes 196616 | tf_op jit(solution)/shard_map/while/body/eval_jaxpr/ppermute | solution.py:13
  276.5 6.2 %collective-permute-start.1 = (f32[1,16,1024]{2,1,0:T(8,128)S(1)}, f32[1,16,1024]{2,1,0:T(8,128)S(1)}, u32[]{:S(2)}, u32[]{:S(2)}) collective-permute-start(f32[1,16,1024]{2,1,0:T(8,128)S(1)} %get-tuple-element.353), channel_id=1, source_target_pairs={{8,0},{16,8},{24,16},{32,24},{40,32},{48,40},{56,48},{64,56},{72,6... | collective-permute-start | bytes 196616 | tf_op jit(solution)/shard_map/while/body/eval_jaxpr/ppermute | solution.py:13
  283.2 5.2 %collective-permute-start = (f32[1,16,1024]{2,1,0:T(8,128)S(1)}, f32[1,16,1024]{2,1,0:T(8,128)S(1)}, u32[]{:S(2)}, u32[]{:S(2)}) collective-permute-start(f32[1,16,1024]{2,1,0:T(8,128)S(1)} %get-tuple-element.352), channel_id=1, source_target_pairs={{0,8},{8,16},{16,24},{24,32},{32,40},{40,48},{48,56},{56,64},{64,7... | collective-permute-start | bytes 196616 | tf_op jit(solution)/shard_map/while/body/eval_jaxpr/ppermute | solution.py:13
  286.5 6.2 %collective-permute-start.1 = (f32[1,16,1024]{2,1,0:T(8,128)S(1)}, f32[1,16,1024]{2,1,0:T(8,128)S(1)}, u32[]{:S(2)}, u32[]{:S(2)}) collective-permute-start(f32[1,16,1024]{2,1,0:T(8,128)S(1)} %get-tuple-element.353), channel_id=1, source_target_pairs={{8,0},{16,8},{24,16},{32,24},{40,32},{48,40},{56,48},{64,56},{72,6... | collective-permute-start | bytes 196616 | tf_op jit(solution)/shard_map/while/body/eval_jaxpr/ppermute | solution.py:13
  293.1 5.0 %collective-permute-start = (f32[1,16,1024]{2,1,0:T(8,128)S(1)}, f32[1,16,1024]{2,1,0:T(8,128)S(1)}, u32[]{:S(2)}, u32[]{:S(2)}) collective-permute-start(f32[1,16,1024]{2,1,0:T(8,128)S(1)} %get-tuple-element.352), channel_id=1, source_target_pairs={{0,8},{8,16},{16,24},{24,32},{32,40},{40,48},{48,56},{56,64},{64,7... | collective-permute-start | bytes 196616 | tf_op jit(solution)/shard_map/while/body/eval_jaxpr/ppermute | solution.py:13
  296.3 6.2 %collective-permute-start.1 = (f32[1,16,1024]{2,1,0:T(8,128)S(1)}, f32[1,16,1024]{2,1,0:T(8,128)S(1)}, u32[]{:S(2)}, u32[]{:S(2)}) collective-permute-start(f32[1,16,1024]{2,1,0:T(8,128)S(1)} %get-tuple-element.353), channel_id=1, source_target_pairs={{8,0},{16,8},{24,16},{32,24},{40,32},{48,40},{56,48},{64,56},{72,6... | collective-permute-start | bytes 196616 | tf_op jit(solution)/shard_map/while/body/eval_jaxpr/ppermute | solution.py:13
  302.9 5.2 %collective-permute-start = (f32[1,16,1024]{2,1,0:T(8,128)S(1)}, f32[1,16,1024]{2,1,0:T(8,128)S(1)}, u32[]{:S(2)}, u32[]{:S(2)}) collective-permute-start(f32[1,16,1024]{2,1,0:T(8,128)S(1)} %get-tuple-element.352), channel_id=1, source_target_pairs={{0,8},{8,16},{16,24},{24,32},{32,40},{40,48},{48,56},{56,64},{64,7... | collective-permute-start | bytes 196616 | tf_op jit(solution)/shard_map/while/body/eval_jaxpr/ppermute | solution.py:13
  306.3 6.2 %collective-permute-start.1 = (f32[1,16,1024]{2,1,0:T(8,128)S(1)}, f32[1,16,1024]{2,1,0:T(8,128)S(1)}, u32[]{:S(2)}, u32[]{:S(2)}) collective-permute-start(f32[1,16,1024]{2,1,0:T(8,128)S(1)} %get-tuple-element.353), channel_id=1, source_target_pairs={{8,0},{16,8},{24,16},{32,24},{40,32},{48,40},{56,48},{64,56},{72,6... | collective-permute-start | bytes 196616 | tf_op jit(solution)/shard_map/while/body/eval_jaxpr/ppermute | solution.py:13
  312.9 5.3 %collective-permute-start = (f32[1,16,1024]{2,1,0:T(8,128)S(1)}, f32[1,16,1024]{2,1,0:T(8,128)S(1)}, u32[]{:S(2)}, u32[]{:S(2)}) collective-permute-start(f32[1,16,1024]{2,1,0:T(8,128)S(1)} %get-tuple-element.352), channel_id=1, source_target_pairs={{0,8},{8,16},{16,24},{24,32},{32,40},{40,48},{48,56},{56,64},{64,7... | collective-permute-start | bytes 196616 | tf_op jit(solution)/shard_map/while/body/eval_jaxpr/ppermute | solution.py:13
  316.4 6.5 %collective-permute-start.1 = (f32[1,16,1024]{2,1,0:T(8,128)S(1)}, f32[1,16,1024]{2,1,0:T(8,128)S(1)}, u32[]{:S(2)}, u32[]{:S(2)}) collective-permute-start(f32[1,16,1024]{2,1,0:T(8,128)S(1)} %get-tuple-element.353), channel_id=1, source_target_pairs={{8,0},{16,8},{24,16},{32,24},{40,32},{48,40},{56,48},{64,56},{72,6... | collective-permute-start | bytes 196616 | tf_op jit(solution)/shard_map/while/body/eval_jaxpr/ppermute | solution.py:13
  323.4 5.3 %collective-permute-start = (f32[1,16,1024]{2,1,0:T(8,128)S(1)}, f32[1,16,1024]{2,1,0:T(8,128)S(1)}, u32[]{:S(2)}, u32[]{:S(2)}) collective-permute-start(f32[1,16,1024]{2,1,0:T(8,128)S(1)} %get-tuple-element.352), channel_id=1, source_target_pairs={{0,8},{8,16},{16,24},{24,32},{32,40},{40,48},{48,56},{56,64},{64,7... | collective-permute-start | bytes 196616 | tf_op jit(solution)/shard_map/while/body/eval_jaxpr/ppermute | solution.py:13
  326.8 6.2 %collective-permute-start.1 = (f32[1,16,1024]{2,1,0:T(8,128)S(1)}, f32[1,16,1024]{2,1,0:T(8,128)S(1)}, u32[]{:S(2)}, u32[]{:S(2)}) collective-permute-start(f32[1,16,1024]{2,1,0:T(8,128)S(1)} %get-tuple-element.353), channel_id=1, source_target_pairs={{8,0},{16,8},{24,16},{32,24},{40,32},{48,40},{56,48},{64,56},{72,6... | collective-permute-start | bytes 196616 | tf_op jit(solution)/shard_map/while/body/eval_jaxpr/ppermute | solution.py:13
  333.5 4.7 %collective-permute-start = (f32[1,16,1024]{2,1,0:T(8,128)S(1)}, f32[1,16,1024]{2,1,0:T(8,128)S(1)}, u32[]{:S(2)}, u32[]{:S(2)}) collective-permute-start(f32[1,16,1024]{2,1,0:T(8,128)S(1)} %get-tuple-element.352), channel_id=1, source_target_pairs={{0,8},{8,16},{16,24},{24,32},{32,40},{40,48},{48,56},{56,64},{64,7... | collective-permute-start | bytes 196616 | tf_op jit(solution)/shard_map/while/body/eval_jaxpr/ppermute | solution.py:13
  336.2 6.2 %collective-permute-start.1 = (f32[1,16,1024]{2,1,0:T(8,128)S(1)}, f32[1,16,1024]{2,1,0:T(8,128)S(1)}, u32[]{:S(2)}, u32[]{:S(2)}) collective-permute-start(f32[1,16,1024]{2,1,0:T(8,128)S(1)} %get-tuple-element.353), channel_id=1, source_target_pairs={{8,0},{16,8},{24,16},{32,24},{40,32},{48,40},{56,48},{64,56},{72,6... | collective-permute-start | bytes 196616 | tf_op jit(solution)/shard_map/while/body/eval_jaxpr/ppermute | solution.py:13
  342.6 1.0 copy-start.2
  416.3 0.7 copy-start.5
